TPU v7x, 32 devices: a whole 2x2x4 slice. The times are simulated.
32 devices in a mesh: groups: 2 (over x), blk: 8 (over z, y), sub: 2 (over core).
Axes of the slice: x: 2, y: 2, z: 4, core: 2. Of those that a mesh axis runs over, the one named last changes fastest.
Arguments:
- queries: bfloat16 [2048, 4096], P(('groups', 'blk'), 'sub'), parts along dimension 0, may hold values from -6 to 6
- passages: bfloat16 [2048, 4096], P(('groups', 'blk'), 'sub'), parts along dimension 0, may hold values from -6 to 6
- negatives: int32 [2048, 7], P(('groups', 'blk')), parts along dimension 0, may hold values from 0 to 1023, as said below
Outputs:
- grad_queries: bfloat16 [2048, 4096], P(('groups', 'blk'), 'sub'), parts along dimension 0
- grad_passages: bfloat16 [2048, 4096], P(('groups', 'blk'), 'sub'), parts along dimension 0
There are 2 independent parts, one for each index of `groups`. A program takes and returns all parts, laid end to end along the dimension named above; each array names one. Nothing has to cross between parts.
Inputs may be any that keep to these rules, and one draw needn't show every extreme that they name: `negatives`: passage j lies in block j // 128. Among the 896 entries of one block of queries (rows of one device along blk), at most 128 name passages of any one block; in every draw some blocks are named exactly 128 times by the entries of every block of queries.
All inputs are finite; a program needn't handle non-finite values.
Results may differ from a plain program's by a relative error of at most 0.005.
Values may be sent and summed in bfloat16 or wider, within the bound.
A program may use at most 64 MiB of HBM per device.

v0:
```python
import math

import jax
import jax.numpy as jnp
from jax import lax
from jax.sharding import PartitionSpec as P

D = 4096
HALF = 2


LOGIT_SLOPE = 2.0
LOGIT_SHIFT = -1.0
HARD_WEIGHT = 2.0


def shifted(value, axis, steps):
    count = lax.axis_size(axis)
    pairs = [(source, (source + steps) % count) for source in range(count)]
    return lax.ppermute(value, axis, pairs)


def tile_step(queries, passage_rows, carried, grad_rows, offset, factor):
    partial_value = jnp.einsum(
        "id,jd->ij", queries, passage_rows, preferred_element_type=jnp.float32
    )
    scores = lax.psum(partial_value, "sub")
    weights = jax.nn.sigmoid(factor * scores + LOGIT_SHIFT)
    if offset == 0:
        weights = weights - jnp.eye(weights.shape[0], dtype=jnp.float32)
    coeffs = weights.astype(jnp.bfloat16)
    grad_rows = grad_rows + jnp.dot(coeffs, passage_rows, preferred_element_type=jnp.float32)
    carried = carried + jnp.einsum("ij,id->jd", coeffs, queries, preferred_element_type=jnp.float32)
    return (carried, grad_rows)


def local(queries, passages, negatives):
    factor = LOGIT_SLOPE / math.sqrt(D)
    row_count, width = queries.shape
    zeros_tile = jnp.zeros((row_count, width), jnp.float32)
    grad_rows = zeros_tile
    upper_block = passages
    lower_block = shifted(passages, "blk", 1)
    upper_accum = zeros_tile
    lower_accum = zeros_tile
    for turn_index in range(HALF + 1):
        upper_accum, grad_rows = tile_step(
            queries, upper_block, upper_accum, grad_rows, turn_index, factor
        )
        if turn_index < HALF:
            lower_accum, grad_rows = tile_step(
                queries, lower_block, lower_accum, grad_rows, -(turn_index + 1), factor
            )
            upper_block = shifted(upper_block, "blk", -1)
            upper_accum = shifted(upper_accum, "blk", -1)
        if turn_index < HALF - 1:
            lower_block = shifted(lower_block, "blk", 1)
            lower_accum = shifted(lower_accum.astype(jnp.bfloat16), "blk", 1).astype(
                lower_accum.dtype
            )
    window_pass = shifted(upper_accum, "blk", HALF) + shifted(lower_accum, "blk", -HALF)
    owners = lax.axis_size("blk")
    neg_count = negatives.shape[1]
    capacity = 8 * row_count // owners
    slot_count = row_count * neg_count
    flat_neg = negatives.reshape(-1)
    owner_of = flat_neg // row_count
    local_row = flat_neg % row_count
    onehot_owner = (owner_of[:, None] == jnp.arange(owners, dtype=jnp.int32)[None, :]).astype(
        jnp.int32
    )
    position = jnp.sum((jnp.cumsum(onehot_owner, axis=0) - 1) * onehot_owner, axis=1)
    slot_index = owner_of * capacity + position
    requests = (
        jnp.full((owners * capacity,), -1, jnp.int32)
        .at[slot_index]
        .set(local_row)
        .reshape(owners, capacity)
    )
    incoming = lax.all_to_all(requests, "blk", split_axis=0, concat_axis=0, tiled=True)
    is_live = incoming >= 0
    picked = jnp.where(is_live, incoming, 0)
    rows_out = jnp.take(passages, picked.reshape(-1), axis=0).reshape(owners, capacity, width)
    fetched = lax.all_to_all(rows_out, "blk", split_axis=0, concat_axis=0, tiled=True)
    slot_rows = jnp.take(fetched.reshape(owners * capacity, width), slot_index, axis=0).reshape(
        row_count, neg_count, width
    )
    hard_partial = jnp.einsum("rkd,rd->rk", slot_rows, queries, preferred_element_type=jnp.float32)
    hard_scores = lax.psum(hard_partial, "sub")
    hard_coeffs = (HARD_WEIGHT * jax.nn.sigmoid(factor * hard_scores + LOGIT_SHIFT)).astype(
        jnp.bfloat16
    )
    grad_rows = grad_rows + jnp.einsum(
        "rk,rkd->rd", hard_coeffs, slot_rows, preferred_element_type=jnp.float32
    )
    source_slot = (
        jnp.zeros((owners * capacity,), jnp.int32)
        .at[slot_index]
        .set(jnp.arange(slot_count, dtype=jnp.int32))
    )
    query_buffer = jnp.take(queries, source_slot // neg_count, axis=0).reshape(
        owners, capacity, width
    )
    arrived_rows = lax.all_to_all(query_buffer, "blk", split_axis=0, concat_axis=0, tiled=True)
    owner_partial = jnp.einsum(
        "scd,scd->sc", arrived_rows, rows_out, preferred_element_type=jnp.float32
    )
    owner_scores = lax.psum(owner_partial, "sub")
    owner_coeffs = jnp.where(
        is_live, HARD_WEIGHT * jax.nn.sigmoid(factor * owner_scores + LOGIT_SHIFT), 0.0
    ).astype(jnp.bfloat16)
    member = (
        jnp.arange(row_count, dtype=jnp.int32)[:, None] == picked.reshape(1, -1)
    ) & is_live.reshape(1, -1)
    weighted = jnp.where(member, owner_coeffs.reshape(1, -1), jnp.zeros((), jnp.bfloat16))
    hard_pass = jnp.dot(
        weighted, arrived_rows.reshape(owners * capacity, width), preferred_element_type=jnp.float32
    )
    grad_queries = (factor * grad_rows).astype(jnp.bfloat16)
    grad_passages = (factor * (window_pass + hard_pass)).astype(jnp.bfloat16)
    return (grad_queries, grad_passages)


def solution(mesh):
    return jax.shard_map(
        local,
        mesh=mesh,
        in_specs=(
            P(("groups", "blk"), "sub"),
            P(("groups", "blk"), "sub"),
            P(("groups", "blk"), None),
        ),
        out_specs=(P(("groups", "blk"), "sub"), P(("groups", "blk"), "sub")),
        check_vma=False,
    )
```

profile of v0, /device:TPU:0, one launch (start us, length us, event | category | flops | bytes accessed | tf_op | source)
XLA Modules:
  0.0 414.6 jit_solution(12146075961652456251)
XLA Ops:
  7.2 0.9 copy.27
  8.0 0.2 reshape.187
  8.2 0.2 reshape.186
  8.4 0.2 reshape.189
  8.7 2.0 reduce-window.6
  10.7 0.1 slice.14
  10.7 0.1 copy.29
  10.9 0.2 reduce-window.9
  11.0 0.1 copy.30
  11.1 0.1 fusion.18
  11.3 5.8 %scatter_custom_fusion = s32[1024]{0:T(1024)} fusion(s32[896]{0:T(1024)S(1)} %fusion.28, s32[896]{0:T(1024)S(1)} %get-tuple-element.14, s32[]{:T(128)} %constant.53.clone.1), kind=kCustom, calls=%fused_computation.94 | custom fusion | bytes 4100 | tf_op jit(solution)/shard_map/scatter | solution.py:77
  17.1 7.3 %all-to-all-start = ((s32[8,1,128]{2,1,0:T(1,128)}), s32[8,1,128]{2,1,0:T(1,128)S(1)}, u32[]{:S(2)}, u32[]{:S(2)}) async-start(s32[8,1,128]{2,1,0:T(1,128)} %bitcast.3), calls=%async_computation | async-start | bytes 8192 | tf_op jit(solution)/shard_map/all_to_all | solution.py:80
  24.4 5.3 %scatter_custom_fusion.1 = s32[1024]{0:T(1024)S(1)} fusion(s32[896]{0:T(1024)S(1)} %fusion.28, s32[896]{0:T(1024)S(1)} %iota.27, s32[]{:T(128)} %constant.50.clone.1), kind=kCustom, calls=%fused_computation.90 | custom fusion | bytes 4100 | tf_op jit(solution)/shard_map/scatter | solution.py:99
  29.7 6.1 %gather_fusion.2 = bf16[1024,2048]{1,0:T(8,128)(2,1)} fusion(bf16[128,2048]{1,0:T(8,128)(2,1)S(1)} %copy-done, s32[1024]{0:T(1024)S(1)} %broadcast_clamp_fusion), kind=kCustom, calls=%fused_computation.1.clone | custom fusion | bytes 8392704 | tf_op jit(solution)/shard_map/jit(_take)/gather | solution.py:101
  35.8 4.6 %broadcast_select_fusion = bf16[1024,2048]{1,0:T(8,128)(2,1)} fusion(bf16[1024,2048]{1,0:T(8,128)(2,1)} %gather_fusion.2, pred[1024]{0:T(1024)(128)(4,1)S(1)} %compare_and_fusion), kind=kLoop, calls=%fused_computation.7 | loop fusion | flops 2097152 | bytes 8389632 | tf_op jit(solution)/shard_map/jit(_take)/select_n | solution.py:101
  40.5 6.1 %all-to-all-start.2 = ((bf16[8,128,2048]{2,1,0:T(8,128)(2,1)}), bf16[8,128,2048]{2,1,0:T(8,128)(2,1)}, u32[]{:S(2)}, u32[]{:S(2)}) async-start(bf16[8,128,2048]{2,1,0:T(8,128)(2,1)} %bitcast.52), calls=%async_computation.2 | async-start | bytes 8388608 | tf_op jit(solution)/shard_map/all_to_all | solution.py:104
  46.6 6.1 %gather_fusion.1 = bf16[1024,2048]{1,0:T(8,128)(2,1)} fusion(bf16[128,2048]{1,0:T(8,128)(2,1)S(1)} %copy-done.1, s32[1024]{0:T(1024)S(1)} %get-tuple-element.13), kind=kCustom, calls=%fused_computation.clone | custom fusion | bytes 8392704 | tf_op jit(solution)/shard_map/jit(_take)/gather | solution.py:83
  52.7 4.6 %broadcast_select_fusion.1 = bf16[1024,2048]{1,0:T(8,128)(2,1)} fusion(bf16[1024,2048]{1,0:T(8,128)(2,1)} %gather_fusion.1, pred[1024]{0:T(1024)(128)(4,1)S(1)} %get-tuple-element.11), kind=kLoop, calls=%fused_computation.8 | loop fusion | flops 2097152 | bytes 8389632 | tf_op jit(solution)/shard_map/jit(_take)/select_n | solution.py:83
  57.3 82.0 %all-to-all-done.2 = bf16[8,128,2048]{2,1,0:T(8,128)(2,1)} async-done(((bf16[8,128,2048]{2,1,0:T(8,128)(2,1)}), bf16[8,128,2048]{2,1,0:T(8,128)(2,1)}, u32[]{:S(2)}, u32[]{:S(2)}) %all-to-all-start.2) | async-done | bytes 4194336 | tf_op jit(solution)/shard_map/all_to_all | solution.py:104
  139.3 4.6 %all-to-all-start.1 = ((bf16[8,128,2048]{2,1,0:T(8,128)(2,1)}), bf16[8,128,2048]{2,1,0:T(8,128)(2,1)}, u32[]{:S(2)}, u32[]{:S(2)}) async-start(bf16[8,128,2048]{2,1,0:T(8,128)(2,1)} %bitcast.50), calls=%async_computation.1 | async-start | bytes 8388608 | tf_op jit(solution)/shard_map/all_to_all | solution.py:84
  143.9 1.9 collective-permute-start
  145.8 2.9 collective-permute-start.1
  148.7 78.3 %collective-permute-done = bf16[128,2048]{1,0:T(8,128)(2,1)S(1)} collective-permute-done((bf16[128,2048]{1,0:T(8,128)(2,1)S(1)}, bf16[128,2048]{1,0:T(8,128)(2,1)S(1)}, u32[]{:S(2)}, u32[]{:S(2)}) %collective-permute-start) | collective-permute-done | bytes 524320 | tf_op jit(solution)/shard_map/ppermute | solution.py:20
  227.0 0.9 fusion.45
  227.9 4.7 %collective-permute-start.3 = (bf16[128,2048]{1,0:T(8,128)(2,1)S(1)}, bf16[128,2048]{1,0:T(8,128)(2,1)S(1)}, u32[]{:S(2)}, u32[]{:S(2)}) collective-permute-start(bf16[128,2048]{1,0:T(8,128)(2,1)S(1)} %collective-permute-done.1), channel_id=1, source_target_pairs={{0,14},{2,0},{4,2},{6,4},{8,6},{10,8},{12,10},{14,12},{1,15},{3,1}... | collective-permute-start | bytes 1572872 | tf_op jit(solution)/shard_map/ppermute | solution.py:20
  232.7 0.9 fusion.46
  233.6 0.9 fusion.47
  234.5 7.1 %collective-permute-done.2 = bf16[128,2048]{1,0:T(8,128)(2,1)S(1)} collective-permute-done((bf16[128,2048]{1,0:T(8,128)(2,1)S(1)}, bf16[128,2048]{1,0:T(8,128)(2,1)S(1)}, u32[]{:S(2)}, u32[]{:S(2)}) %collective-permute-start.2) | collective-permute-done | bytes 524320 | tf_op jit(solution)/shard_map/ppermute | solution.py:20
  241.7 0.9 fusion.48
  242.6 8.4 %collective-permute-done.3 = bf16[128,2048]{1,0:T(8,128)(2,1)S(1)} collective-permute-done((bf16[128,2048]{1,0:T(8,128)(2,1)S(1)}, bf16[128,2048]{1,0:T(8,128)(2,1)S(1)}, u32[]{:S(2)}, u32[]{:S(2)}) %collective-permute-start.3) | collective-permute-done | bytes 524320 | tf_op jit(solution)/shard_map/ppermute | solution.py:20
  251.0 0.9 fusion.49
  251.9 0.2 reduce_sum.14
  252.1 0.1 copy.31
  252.2 39.4 %all-reduce.4.cloned.1.call-done = (f32[128,128]{1,0:T(8,128)}, f32[128,128]{1,0:T(8,128)}, f32[128,128]{1,0:T(8,128)}, f32[128,128]{1,0:T(8,128)}, f32[128,128]{1,0:T(8,128)}) async-done(((f32[128,128]{1,0:T(8,128)}, f32[128,128]{1,0:T(8,128)}, f32[128,128]{1,0:T(8,128)}, f32[128,128]{1,0:T(8,128)}, f32[128,128]{1,0:T(8,128)}), (f32[128,128]{1,0:T(8,128)}, f32[128,128]{1,0:T(8,128)}, f32[128,128]{1,0:T(8,128)}, ...) | async-done | bytes 327696 | tf_op jit(solution)/shard_map/psum | solution.py:27
  291.5 2.2 fusion.43
  293.7 4.6 %collective-permute-start.4 = (f32[128,2048]{1,0:T(8,128)}, f32[128,2048]{1,0:T(8,128)}, u32[]{:S(2)}, u32[]{:S(2)}) collective-permute-start(f32[128,2048]{1,0:T(8,128)} %fusion.43), channel_id=1, source_target_pairs={{0,14},{2,0},{4,2},{6,4},{8,6},{10,8},{12,10},{14,12},{1,15},{3,1}... | collective-permute-start | bytes 3145736 | tf_op jit(solution)/shard_map/ppermute | solution.py:20
  298.3 0.1 copy.32
  298.5 1.2 convolution_convert_fusion
  299.7 1.1 fusion.44
  300.9 0.3 convolution_add_fusion.3
  301.2 29.5 %collective-permute-done.4 = f32[128,2048]{1,0:T(8,128)} collective-permute-done((f32[128,2048]{1,0:T(8,128)}, f32[128,2048]{1,0:T(8,128)}, u32[]{:S(2)}, u32[]{:S(2)}) %collective-permute-start.4) | collective-permute-done | bytes 1048608 | tf_op jit(solution)/shard_map/ppermute | solution.py:20
  330.7 1.6 convolution_add_fusion
  332.3 2.6 collective-permute-start.5
  335.0 0.3 fusion.41
  335.3 0.3 fusion.42
  335.6 0.3 convolution_add_fusion.2
  335.9 1.3 convert_add_fusion
  337.3 1.0 collective-permute-start.8
  338.3 20.3 %collective-permute-done.5 = f32[128,2048]{1,0:T(8,128)S(1)} collective-permute-done((f32[128,2048]{1,0:T(8,128)S(1)}, f32[128,2048]{1,0:T(8,128)S(1)}, u32[]{:S(2)}, u32[]{:S(2)}) %collective-permute-start.5) | collective-permute-done | bytes 1048608 | tf_op jit(solution)/shard_map/ppermute | solution.py:20
  358.6 1.1 add.188
  359.7 0.2 collective-permute-start.6
  359.8 3.4 fusion
  363.3 11.5 %gather_fusion = bf16[896,2048]{1,0:T(8,128)(2,1)} fusion(bf16[1024,2048]{1,0:T(8,128)(2,1)} %bitcast.6, s32[1024]{0:T(1024)S(1)} %pad_clamp_fusion), kind=kCustom, calls=%fused_computation.2 | custom fusion | bytes 7343616 | tf_op jit(solution)/shard_map/jit(_take)/gather | solution.py:85
  374.8 6.1 %gather.10 = bf16[128,7,2048]{2,1,0:T(8,128)(2,1)} reshape(bf16[896,2048]{1,0:T(8,128)(2,1)} %gather_fusion) | data formatting | bytes 7340032 | tf_op jit(solution)/shard_map/jit(_take)/gather | solution.py:85
  380.9 5.4 %fusion.2 = f32[128,1,7]{2,1,0:T(1,128)S(1)} fusion(bf16[128,7,2048]{2,1,0:T(8,128)(2,1)} %gather.10, pred[128,7]{1,0:T(8,128)(4,1)S(1)} %copy.32, bf16[128,2048,1]{1,0,2:T(8,128)(2,1)S(1)} %bitcast.49), kind=kOutput, calls=%fused_computation.11 | convolution fusion | flops 5505024 | bytes 4198784 | tf_op jit(solution)/shard_map/rkd,rd->rk/dot_general | solution.py:88
  386.3 0.1 copy.36
  386.4 2.5 all-reduce
  388.9 0.1 copy.37
  389.1 3.1 fusion.12
  392.2 0.4 copy-done.3
  392.5 1.3 fusion.1
  393.9 10.0 %collective-permute-done.6 = f32[128,2048]{1,0:T(8,128)} collective-permute-done((f32[128,2048]{1,0:T(8,128)}, f32[128,2048]{1,0:T(8,128)}, u32[]{:S(2)}, u32[]{:S(2)}) %collective-permute-start.6) | collective-permute-done | bytes 1048608 | tf_op jit(solution)/shard_map/ppermute | solution.py:20
  403.9 2.5 multiply_convert_fusion
  406.4 1.3 fusion.6
  (43 shorter events, 0.3 us)
Async XLA Ops:
  7.2 22.6 %copy-start = (bf16[128,2048]{1,0:T(8,128)(2,1)S(1)}, bf16[128,2048]{1,0:T(8,128)(2,1)}, u32[]{:S(2)}) copy-start(bf16[128,2048]{1,0:T(8,128)(2,1)} %param.5) | copy-start | bytes 1572868
  17.1 23.3 %all-to-all-start = ((s32[8,1,128]{2,1,0:T(1,128)}), s32[8,1,128]{2,1,0:T(1,128)S(1)}, u32[]{:S(2)}, u32[]{:S(2)}) async-start(s32[8,1,128]{2,1,0:T(1,128)} %bitcast.3), calls=%async_computation | async-start | bytes 8192 | tf_op jit(solution)/shard_map/all_to_all | solution.py:80
  40.4 6.1 %copy-start.1 = (bf16[128,2048]{1,0:T(8,128)(2,1)S(1)}, bf16[128,2048]{1,0:T(8,128)(2,1)}, u32[]{:S(2)}) copy-start(bf16[128,2048]{1,0:T(8,128)(2,1)} %param.6) | copy-start | bytes 1572868
  40.5 98.8 %all-to-all-start.2 = ((bf16[8,128,2048]{2,1,0:T(8,128)(2,1)}), bf16[8,128,2048]{2,1,0:T(8,128)(2,1)}, u32[]{:S(2)}, u32[]{:S(2)}) async-start(bf16[8,128,2048]{2,1,0:T(8,128)(2,1)} %bitcast.52), calls=%async_computation.2 | async-start | bytes 8388608 | tf_op jit(solution)/shard_map/all_to_all | solution.py:104
  139.3 224.0 %all-to-all-start.1 = ((bf16[8,128,2048]{2,1,0:T(8,128)(2,1)}), bf16[8,128,2048]{2,1,0:T(8,128)(2,1)}, u32[]{:S(2)}, u32[]{:S(2)}) async-start(bf16[8,128,2048]{2,1,0:T(8,128)(2,1)} %bitcast.50), calls=%async_computation.1 | async-start | bytes 8388608 | tf_op jit(solution)/shard_map/all_to_all | solution.py:84
  143.9 154.5 %copy-start.10 = (s32[128,7]{0,1:T(8,128)S(1)}, s32[128,7]{0,1:T(8,128)}, u32[]{:S(2)}) copy-start(s32[128,7]{0,1:T(8,128)} %param.7) | copy-start | bytes 10756
  143.9 147.7 %all-reduce.4.cloned.1.call-start = ((), (), s32[]{:S(2)}) async-start(), calls=%async_computation.3 | async-start | bytes 655360 | tf_op jit(solution)/shard_map/psum | solution.py:27
  143.9 83.1 %collective-permute-start = (bf16[128,2048]{1,0:T(8,128)(2,1)S(1)}, bf16[128,2048]{1,0:T(8,128)(2,1)S(1)}, u32[]{:S(2)}, u32[]{:S(2)}) collective-permute-start(bf16[128,2048]{1,0:T(8,128)(2,1)S(1)} %copy-done.1), channel_id=1, source_target_pairs={{0,2},{2,4},{4,6},{6,8},{8,10},{10,12},{12,14},{14,0},{1,3},{3,5},... | collective-permute-start | bytes 1572872 | tf_op jit(solution)/shard_map/ppermute | solution.py:20
  145.8 82.1 %collective-permute-start.1 = (bf16[128,2048]{1,0:T(8,128)(2,1)S(1)}, bf16[128,2048]{1,0:T(8,128)(2,1)S(1)}, u32[]{:S(2)}, u32[]{:S(2)}) collective-permute-start(bf16[128,2048]{1,0:T(8,128)(2,1)S(1)} %copy-done.1), channel_id=1, source_target_pairs={{0,14},{2,0},{4,2},{6,4},{8,6},{10,8},{12,10},{14,12},{1,15},{3,1}... | collective-permute-start | bytes 1572872 | tf_op jit(solution)/shard_map/ppermute | solution.py:20
  227.0 14.7 %collective-permute-start.2 = (bf16[128,2048]{1,0:T(8,128)(2,1)S(1)}, bf16[128,2048]{1,0:T(8,128)(2,1)S(1)}, u32[]{:S(2)}, u32[]{:S(2)}) collective-permute-start(bf16[128,2048]{1,0:T(8,128)(2,1)S(1)} %collective-permute-done), channel_id=1, source_target_pairs={{0,2},{2,4},{4,6},{6,8},{8,10},{10,12},{12,14},{14,0},{1,3},{3,5},... | collective-permute-start | bytes 1572872 | tf_op jit(solution)/shard_map/ppermute | solution.py:20
  227.9 23.0 %collective-permute-start.3 = (bf16[128,2048]{1,0:T(8,128)(2,1)S(1)}, bf16[128,2048]{1,0:T(8,128)(2,1)S(1)}, u32[]{:S(2)}, u32[]{:S(2)}) collective-permute-start(bf16[128,2048]{1,0:T(8,128)(2,1)S(1)} %collective-permute-done.1), channel_id=1, source_target_pairs={{0,14},{2,0},{4,2},{6,4},{8,6},{10,8},{12,10},{14,12},{1,15},{3,1}... | collective-permute-start | bytes 1572872 | tf_op jit(solution)/shard_map/ppermute | solution.py:20
  241.7 59.5 %copy-start.4 = (bf16[128,2048]{1,0:T(8,128)(2,1)}, bf16[128,2048]{1,0:T(8,128)(2,1)S(1)}, u32[]{:S(2)}) copy-start(bf16[128,2048]{1,0:T(8,128)(2,1)S(1)} %collective-permute-done.2) | copy-start | bytes 1572868
  291.5 9.3 %copy-start.8 = (f32[128,128]{1,0:T(8,128)S(1)}, f32[128,128]{1,0:T(8,128)}, u32[]{:S(2)}) copy-start(f32[128,128]{1,0:T(8,128)} %get-tuple-element.7) | copy-start | bytes 196612
  291.5 39.2 %copy-start.9 = (f32[128,128]{1,0:T(8,128)S(1)}, f32[128,128]{1,0:T(8,128)}, u32[]{:S(2)}) copy-start(f32[128,128]{1,0:T(8,128)} %get-tuple-element.8) | copy-start | bytes 196612
  293.7 41.2 %copy-start.7 = (f32[128,128]{1,0:T(8,128)S(1)}, f32[128,128]{1,0:T(8,128)}, u32[]{:S(2)}) copy-start(f32[128,128]{1,0:T(8,128)} %get-tuple-element.5) | copy-start | bytes 196612
  293.7 37.0 %collective-permute-start.4 = (f32[128,2048]{1,0:T(8,128)}, f32[128,2048]{1,0:T(8,128)}, u32[]{:S(2)}, u32[]{:S(2)}) collective-permute-start(f32[128,2048]{1,0:T(8,128)} %fusion.43), channel_id=1, source_target_pairs={{0,14},{2,0},{4,2},{6,4},{8,6},{10,8},{12,10},{14,12},{1,15},{3,1}... | collective-permute-start | bytes 3145736 | tf_op jit(solution)/shard_map/ppermute | solution.py:20
  299.7 36.2 %collective-permute-start.7 = (bf16[128,2048]{1,0:T(8,128)(2,1)S(1)}, bf16[128,2048]{1,0:T(8,128)(2,1)S(1)}, u32[]{:S(2)}, u32[]{:S(2)}) collective-permute-start(bf16[128,2048]{1,0:T(8,128)(2,1)S(1)} %convolution_convert_fusion), channel_id=1, source_target_pairs={{0,2},{2,4},{4,6},{6,8},{8,10},{10,12},{12,14},{14,0},{1,3},{3,5},... | collective-permute-start | bytes 1572872 | tf_op jit(solution)/shard_map/ppermute | solution.py:20
  330.7 5.2 %copy-start.6 = (f32[128,128]{1,0:T(8,128)S(1)}, f32[128,128]{1,0:T(8,128)}, u32[]{:S(2)}) copy-start(f32[128,128]{1,0:T(8,128)} %get-tuple-element.9) | copy-start | bytes 196612
  332.3 26.2 %collective-permute-start.5 = (f32[128,2048]{1,0:T(8,128)S(1)}, f32[128,2048]{1,0:T(8,128)S(1)}, u32[]{:S(2)}, u32[]{:S(2)}) collective-permute-start(f32[128,2048]{1,0:T(8,128)S(1)} %convolution_add_fusion), channel_id=1, source_target_pairs={{0,14},{2,0},{4,2},{6,4},{8,6},{10,8},{12,10},{14,12},{1,15},{3,1}... | collective-permute-start | bytes 3145736 | tf_op jit(solution)/shard_map/ppermute | solution.py:20
  335.6 24.2 %copy-start.2 = (bf16[1024,2048]{1,0:T(8,128)(2,1)S(1)}, bf16[1024,2048]{1,0:T(8,128)(2,1)}, u32[]{:S(2)}) copy-start(bf16[1024,2048]{1,0:T(8,128)(2,1)} %broadcast_select_fusion.1) | copy-start | bytes 12582916
  337.3 56.6 %collective-permute-start.8 = (f32[128,2048]{1,0:T(8,128)}, f32[128,2048]{1,0:T(8,128)}, u32[]{:S(2)}, u32[]{:S(2)}) collective-permute-start(f32[128,2048]{1,0:T(8,128)} %convert_add_fusion), channel_id=1, source_target_pairs={{0,12},{2,14},{4,0},{6,2},{8,4},{10,6},{12,8},{14,10},{1,13},{3,15... | collective-permute-start | bytes 3145736 | tf_op jit(solution)/shard_map/ppermute | solution.py:20
  359.7 44.2 %collective-permute-start.6 = (f32[128,2048]{1,0:T(8,128)}, f32[128,2048]{1,0:T(8,128)}, u32[]{:S(2)}, u32[]{:S(2)}) collective-permute-start(f32[128,2048]{1,0:T(8,128)} %add.188), channel_id=1, source_target_pairs={{0,4},{2,6},{4,8},{6,10},{8,12},{10,14},{12,0},{14,2},{1,5},{3,7},... | collective-permute-start | bytes 3145736 | tf_op jit(solution)/shard_map/ppermute | solution.py:20
  389.1 3.5 copy-start.3
  392.5 13.9 %copy-start.5 = (bf16[128,2048]{1,0:T(8,128)(2,1)S(1)}, bf16[128,2048]{1,0:T(8,128)(2,1)}, u32[]{:S(2)}) copy-start(bf16[128,2048]{1,0:T(8,128)(2,1)} %copy-done.4) | copy-start | bytes 1572868
Sparse Core Ops, SparseCore 0:
  252.0 39.4 all-reduce.3
where the time goes:
time: 415 us
  waiting for transfers between devices  275 us (66%)
  local copies, waits for them, and re-layouts  43.7 us (11%)
  starting transfers between devices  36 us (9%)
  matrix products  24.5 us (6%)
  other arithmetic  18.7 us (5%)
  between operations  14.3 us (3%)
    ppermute x9, waiting for transfers between devices, shifted(): return lax.ppermute(value, axis, pairs)  154 us
    all_to_all x1, waiting for transfers between devices, local(): lax.all_to_all(query_buffer, 'blk', split_axis=0, concat_axis=0, tiled=True)  82 us
    psum x1, waiting for transfers between devices, tile_step(): scores = lax.psum(partial_value, 'sub')  39.4 us
    ppermute x9, starting transfers between devices, shifted(): return lax.ppermute(value, axis, pairs)  18 us
    gather x2, local copies, waits for them, and re-layouts, local(): jnp.take(fetched.reshape(owners * capacity, width), slot_index, axis=0)  17.6 us
  transfers between devices with their start and end apart: 13, of which 8 were waited for; matrix products, arithmetic and copies ran while one was open for 18% of the time, Pallas kernels for 0%

commit v1 on v0

--- a/solution.py
+++ b/solution.py
@@ -121,9 +121,48 @@
     return (grad_queries, grad_passages)
 
 
+def pair_weights(scores, counts, near, diagonal, factor):
+    gate = jax.nn.sigmoid(factor * scores + LOGIT_SHIFT)
+    window = jnp.where(near, gate - diagonal, 0.0).astype(jnp.bfloat16).astype(jnp.float32)
+    hard = (HARD_WEIGHT * gate).astype(jnp.bfloat16).astype(jnp.float32)
+    return (window + counts * hard).astype(jnp.bfloat16)
+
+
+def dense_local(queries, passages, negatives):
+    factor = LOGIT_SLOPE / math.sqrt(D)
+    row_count, width = queries.shape
+    owners = lax.axis_size("blk")
+    me = lax.axis_index("blk")
+    total = owners * row_count
+    all_passages = lax.all_gather(passages, "blk", axis=0, tiled=True)
+    all_queries = lax.all_gather(queries, "blk", axis=0, tiled=True)
+    all_negatives = lax.all_gather(negatives, "blk", axis=0, tiled=True)
+    row_part = jnp.einsum("id,jd->ij", queries, all_passages, preferred_element_type=jnp.float32)
+    col_part = jnp.einsum("jd,id->ji", passages, all_queries, preferred_element_type=jnp.float32)
+    row_scores, col_scores = lax.psum((row_part, col_part), "sub")
+    mine = me * row_count + lax.broadcasted_iota(jnp.int32, (row_count, total), 0)
+    other = lax.broadcasted_iota(jnp.int32, (row_count, total), 1)
+    gap = (other // row_count - me + HALF + owners) % owners
+    near = gap <= 2 * HALF
+    diagonal = (mine == other).astype(jnp.float32)
+    row_counts = jnp.zeros((row_count, total), jnp.float32)
+    col_counts = jnp.zeros((row_count, total), jnp.float32)
+    turned = all_negatives.T
+    for k in range(negatives.shape[1]):
+        row_counts += (negatives[:, k : k + 1] == other).astype(jnp.float32)
+        col_counts += (turned[k : k + 1, :] == mine).astype(jnp.float32)
+    row_w = pair_weights(row_scores, row_counts, near, diagonal, factor)
+    col_w = pair_weights(col_scores, col_counts, near, diagonal, factor)
+    grad_queries = factor * jnp.dot(row_w, all_passages, preferred_element_type=jnp.float32)
+    grad_passages = factor * jnp.dot(col_w, all_queries, preferred_element_type=jnp.float32)
+    return (grad_queries.astype(jnp.bfloat16), grad_passages.astype(jnp.bfloat16))
+
+
 def solution(mesh):
+    owners = mesh.shape["blk"]
+    body = dense_local if owners == 8 else local
     return jax.shard_map(
-        local,
+        body,
         mesh=mesh,
         in_specs=(
             P(("groups", "blk"), "sub"),

time: 415 us -> 209 us (0.50)
  waiting for transfers between devices: 275 us -> 148 us
  local copies, waits for them, and re-layouts: 43.7 us -> 0.05 us
  starting transfers between devices: 36 us -> 0.11 us
  blocking collectives: 2.48 us -> 30.4 us
  other arithmetic: 18.7 us -> 0.02 us
  matrix products: 24.5 us -> 15.9 us
    ppermute x9 -> x0, waiting for transfers between devices: 154 us -> none  [shifted(): return lax.ppermute(value, axis, pairs)]
    all_gather x0 -> x2, waiting for transfers between devices: none -> 147 us  [the longest x1 77.6 us: dense_local(): all_passages = lax.all_gather(passages, 'blk', axis=0, tiled=True)]
    all_to_all x3 -> x0, waiting for transfers between devices: 82 us -> none  [the longest x1 82 us: local(): lax.all_to_all(query_buffer, 'blk', split_axis=0, concat_axis=0, tiled=True)]
    psum x1, waiting for transfers between devices: 39.4 us -> 0.02 us  [dense_local(): row_scores, col_scores = lax.psum((row_part, col_part), 'sub')]
    all_gather x0 -> x1, blocking collectives: none -> 30.4 us  [dense_local(): all_negatives = lax.all_gather(negatives, 'blk', axis=0, tiled=True)]
    gather x4 -> x0, local copies, waits for them, and re-layouts: 29.8 us -> none  [the longest x2 17.6 us: local(): jnp.take(fetched.reshape(owners * capacity, width), slot_index, axis=0)]
    all_to_all x3 -> x0, starting transfers between devices: 18 us -> none  [the longest x1 7.28 us: local(): lax.all_to_all(requests, 'blk', split_axis=0, concat_axis=0, tiled=True)]
    ppermute x9 -> x0, starting transfers between devices: 18 us -> none  [shifted(): return lax.ppermute(value, axis, pairs)]
  transfers between devices with their start and end apart: 13 -> 3, of which waited for: 8 -> 2; matrix products, arithmetic and copies ran while one was open for 18% -> 2% of each run, Pallas kernels for 0% -> 0%
where the time goes in v1:
time: 209 us; the launch traced here: 208 us
  waiting for transfers between devices  148 us (71%)
  blocking collectives  30.4 us (15%)
  matrix products  15.9 us (8%)
  between operations  13.8 us (7%)
    all_gather x1, waiting for transfers between devices, dense_local(): all_passages = lax.all_gather(passages, 'blk', axis=0, tiled=True)  77.6 us
    all_gather x1, waiting for transfers between devices, dense_local(): all_queries = lax.all_gather(queries, 'blk', axis=0, tiled=True)  69.1 us
    all_gather x1, blocking collectives, dense_local(): all_negatives = lax.all_gather(negatives, 'blk', axis=0, tiled=True)  30.4 us
    dot_general x1, matrix products, dense_local(): jnp.dot(row_w, all_passages, preferred_element_type=jnp.float32)  4.69 us
    dot_general x1, matrix products, dense_local(): jnp.einsum('id,jd->ij', queries, all_passages, preferred_element_type=jnp...  4.67 us
    dot_general x1, matrix products, dense_local(): jnp.einsum('jd,id->ji', passages, all_queries, preferred_element_type=jnp...  4.49 us
  transfers between devices with their start and end apart: 3, of which 2 were waited for; matrix products, arithmetic and copies ran while one was open for 2% of the time, Pallas kernels for 0%

profile of v1, /device:TPU:0, one launch (start us, length us, event | category | flops | bytes accessed | tf_op | source)
XLA Modules:
  0.0 208.4 jit_solution(11236755315703884727)
XLA Ops:
  7.2 0.0 copy-start.1
  7.2 0.0 all-gather.3.cloned.1.call-start
  7.2 0.7 all-gather.3.cloned.1.call-update
  7.9 0.0 all-gather.5.cloned.1.call-start
  8.0 0.7 all-gather.5.cloned.1.call-update
  8.7 0.0 all-reduce.3.cloned.1.call-start
  8.7 77.6 %all-gather.3.cloned.1.call-done = bf16[1024,2048]{1,0:T(8,128)(2,1)} async-done(((bf16[128,2048]{1,0:T(8,128)(2,1)}), bf16[1024,2048]{1,0:T(8,128)(2,1)}) %all-gather.3.cloned.1.call-update) | async-done | bytes 4194320 | tf_op jit(solution)/shard_map/all_gather | solution.py:137
  86.3 4.7 %fusion.62 = f32[128,1024]{1,0:T(8,128)} fusion(bf16[128,2048]{1,0:T(8,128)(2,1)} %param.3, bf16[1024,2048]{1,0:T(8,128)(2,1)} %all-gather.3.cloned.1.call-done), kind=kOutput, calls=%fused_computation.91 | convolution fusion | flops 536870912 | bytes 5242880 | tf_op jit(solution)/shard_map/id,jd->ij/dot_general | solution.py:140
  90.9 0.0 copy-start.2
  90.9 69.1 %all-gather.5.cloned.1.call-done = bf16[1024,2048]{1,0:T(8,128)(2,1)} async-done(((bf16[128,2048]{1,0:T(8,128)(2,1)}), bf16[1024,2048]{1,0:T(8,128)(2,1)}) %all-gather.5.cloned.1.call-update) | async-done | bytes 4194320 | tf_op jit(solution)/shard_map/all_gather | solution.py:138
  160.1 0.0 copy-done.1
  160.1 4.5 %fusion.63 = f32[128,1024]{1,0:T(8,128)} fusion(bf16[128,2048]{1,0:T(8,128)(2,1)S(1)} %copy-done.1, bf16[1024,2048]{1,0:T(8,128)(2,1)} %all-gather.5.cloned.1.call-done), kind=kOutput, calls=%fused_computation.92 | convolution fusion | flops 536870912 | bytes 5242880 | tf_op jit(solution)/shard_map/jd,id->ji/dot_general | solution.py:141
  164.6 0.0 all-reduce.3.cloned.1.call-update
  164.6 0.0 copy-done.2
  164.6 30.4 %all_gather.11 = s32[1024,7]{0,1:T(8,128)S(1)} all-gather(s32[128,7]{0,1:T(8,128)S(1)} %copy-done.2), channel_id=1, replica_groups=mesh['groups'=2,'blk'=8,'sub'=2] {'blk'}, dimensions={0}, use_global_device_ids=true | all-gather | bytes 32256 | tf_op jit(solution)/shard_map/all_gather | solution.py:139
  195.1 0.0 all-reduce.3.cloned.1.call-done
  195.1 0.0 copy-start
  195.1 0.0 copy-start.3
  195.2 4.7 %fusion = bf16[128,2048]{1,0:T(8,128)(2,1)} fusion(bf16[1024,2048]{1,0:T(8,128)(2,1)} %all-gather.3.cloned.1.call-done, f32[128,1024]{1,0:T(8,128)} %get-tuple-element.2, s32[128]{0:T(128)S(1)} %get-tuple-element.17, s32[128]{0:T(128)S(1)} %get-tuple-element.12, s32[128]{0:T(128)S(1)} %get-tuple-element.13, s32[128]{0:T(128)S(1)} %get-tuple-element.14, ...), kind=kOutput, calls=%fused_computation.2 | convolution fusion | flops 544210944 | bytes 5256196 | tf_op jit(solution)/shard_map/dot_general | solution.py:156
  199.8 0.0 copy-done
  199.8 0.0 copy-done.3
  199.8 2.1 fusion.1
  (5 shorter events, 0.0 us)
Async XLA Ops:
  7.2 152.9 %copy-start.1 = (bf16[128,2048]{1,0:T(8,128)(2,1)S(1)}, bf16[128,2048]{1,0:T(8,128)(2,1)}, u32[]{:S(2)}) copy-start(bf16[128,2048]{1,0:T(8,128)(2,1)} %param.4) | copy-start | bytes 1572868
  7.2 79.1 %all-gather.3.cloned.1.call-start = ((), (), s32[]{:S(2)}) async-start(), calls=%async_computation | async-start | bytes 4718592 | tf_op jit(solution)/shard_map/all_gather | solution.py:137
  7.9 152.2 %all-gather.5.cloned.1.call-start = ((), (), s32[]{:S(2)}) async-start(), calls=%async_computation.1 | async-start | bytes 4718592 | tf_op jit(solution)/shard_map/all_gather | solution.py:138
  8.7 186.5 %all-reduce.3.cloned.1.call-start = ((), (), s32[]{:S(2)}) async-start(), calls=%async_computation.2 | async-start | bytes 2097152 | tf_op jit(solution)/shard_map/psum | solution.py:142
  90.9 73.7 %copy-start.2 = (s32[128,7]{0,1:T(8,128)S(1)}, s32[128,7]{0,1:T(8,128)}, u32[]{:S(2)}) copy-start(s32[128,7]{0,1:T(8,128)} %param.5) | copy-start | bytes 10756
  195.1 4.7 %copy-start = (bf16[1024,2048]{1,0:T(8,128)(2,1)S(1)}, bf16[1024,2048]{1,0:T(8,128)(2,1)}, u32[]{:S(2)}) copy-start(bf16[1024,2048]{1,0:T(8,128)(2,1)} %all-gather.5.cloned.1.call-done) | copy-start | bytes 12582916
  195.1 4.7 %copy-start.3 = (f32[128,1024]{1,0:T(8,128)S(1)}, f32[128,1024]{1,0:T(8,128)}, u32[]{:S(2)}) copy-start(f32[128,1024]{1,0:T(8,128)} %get-tuple-element.3) | copy-start | bytes 1572868
Sparse Core Ops, SparseCore 0:
  10.1 76.0 all-gather.2
  88.4 71.6 all-gather.4
  164.7 17.9 all-reduce.2

commit v2 on v0

--- a/solution.py
+++ b/solution.py
@@ -1,8 +1,11 @@
+import functools
 import math
 
 import jax
 import jax.numpy as jnp
 from jax import lax
+from jax.experimental import pallas as pl
+from jax.experimental.pallas import tpu as pltpu
 from jax.sharding import PartitionSpec as P
 
 D = 4096
@@ -121,9 +124,303 @@
     return (grad_queries, grad_passages)
 
 
+def pair_weights(scores, counts, near, diagonal, factor):
+    gate = jax.nn.sigmoid(factor * scores + LOGIT_SHIFT)
+    window = jnp.where(near, gate - diagonal, 0.0).astype(jnp.bfloat16).astype(jnp.float32)
+    hard = (HARD_WEIGHT * gate).astype(jnp.bfloat16).astype(jnp.float32)
+    return (window + counts * hard).astype(jnp.bfloat16)
+
+
+CHUNKS = 8
+EARLY = 7
+TILE = 512
+
+
+def line_kernel(
+    owners, neg_count, q_hbm, p_hbm, neg_ref, turned_ref, gq_ref, gp_ref,
+    held, turned_all, own_part, other_part, row_w, col_w,
+    load_sem, neg_send, neg_recv, up_send, down_send, cross_send, recv_sem, score_sem,
+):
+    factor = LOGIT_SLOPE / math.sqrt(D)
+    row_count = q_hbm.shape[0]
+    width = q_hbm.shape[1]
+    chunk_rows = 2 * row_count // CHUNKS
+    half = CHUNKS // 2
+    line = owners // 2
+    me = lax.axis_index("blk")
+    side = lax.axis_index("sub")
+    place = me // 2
+    lane = me % 2
+    partner = place * 2 + 1 - lane
+
+    def chunk(block, piece):
+        start = pl.multiple_of(block * row_count + (piece % half) * chunk_rows, chunk_rows)
+        return held.at[piece // half, pl.ds(start, chunk_rows), :]
+
+    def send(block, piece, sems, target):
+        return pltpu.make_async_remote_copy(
+            src_ref=chunk(block, piece), dst_ref=chunk(block, piece),
+            send_sem=sems.at[block, piece], recv_sem=recv_sem.at[block, piece],
+            device_id={"blk": target}, device_id_type=pl.DeviceIdType.MESH,
+        )
+
+    def upward(block, piece):
+        return send(block, piece, up_send, me + 2)
+
+    def downward(block, piece):
+        return send(block, piece, down_send, me - 2)
+
+    def across(block, piece):
+        return send(block, piece, cross_send, partner)
+
+    def arrived(block, piece):
+        send(block, piece, cross_send, partner).wait_recv()
+
+    own_rows = pl.ds(pl.multiple_of(me * row_count, row_count), row_count)
+    loads = [
+        pltpu.make_async_copy(q_hbm, held.at[0, own_rows, :], load_sem.at[0]),
+        pltpu.make_async_copy(p_hbm, held.at[1, own_rows, :], load_sem.at[1]),
+    ]
+    for load in loads:
+        load.start()
+    barrier = pltpu.get_barrier_semaphore()
+    for step in range(1, owners):
+        pl.semaphore_signal(
+            barrier, inc=1, device_id={"blk": (me + step) % owners},
+            device_id_type=pl.DeviceIdType.MESH,
+        )
+    pl.semaphore_signal(
+        barrier, inc=1, device_id={"sub": 1 - side}, device_id_type=pl.DeviceIdType.MESH
+    )
+    turned_all[me] = turned_ref[...]
+    for load in loads:
+        load.wait()
+    pl.semaphore_wait(barrier, owners)
+
+    @pl.loop(0, CHUNKS)
+    def _(piece):
+        @pl.when(place < line - 1)
+        def _():
+            upward(me, piece).start()
+
+        @pl.when(place > 0)
+        def _():
+            downward(me, piece).start()
+
+        across(me, piece).start()
+
+    def neg_copy(step):
+        return pltpu.make_async_remote_copy(
+            src_ref=turned_all.at[me], dst_ref=turned_all.at[me],
+            send_sem=neg_send.at[step], recv_sem=neg_recv.at[me],
+            device_id={"blk": (me + step) % owners}, device_id_type=pl.DeviceIdType.MESH,
+        )
+
+    for step in range(1, owners):
+        neg_copy(step).start()
+
+    @pl.loop(EARLY, CHUNKS)
+    def _(piece):
+        arrived(partner, piece)
+
+        @pl.when(place < line - 1)
+        def _():
+            upward(partner, piece).start()
+
+        @pl.when(place > 0)
+        def _():
+            downward(partner, piece).start()
+
+    for far in range(1, line):
+        below = (place - far) * 2
+        above = (place + far) * 2
+
+        def forward(piece, row, cross):
+            @pl.when(place >= far)
+            def _():
+                block = below + row
+                arrived(block, piece)
+
+                @pl.when(place < line - 1)
+                def _():
+                    upward(block, piece).start()
+
+                if cross:
+                    across(block, piece).start()
+
+            @pl.when(place + far < line)
+            def _():
+                block = above + row
+                arrived(block, piece)
+
+                @pl.when(place > 0)
+                def _():
+                    downward(block, piece).start()
+
+                if cross:
+                    across(block, piece).start()
+
+        @pl.loop(0, EARLY)
+        def _(piece):
+            forward(piece, lane, True)
+
+        @pl.loop(EARLY, CHUNKS)
+        def _(piece):
+            forward(piece, lane, False)
+
+        @pl.loop(EARLY, CHUNKS)
+        def _(piece):
+            forward(piece, 1 - lane, False)
+
+    @pl.loop(0, line)
+    def _(spot):
+        @pl.loop(0, EARLY)
+        def _(piece):
+            arrived(spot * 2 + 1 - lane, piece)
+
+    @pl.loop(0, owners)
+    def _(block):
+        rows = pl.ds(pl.multiple_of(block * row_count, row_count), row_count)
+        own_part[0, block] = lax.dot_general(
+            held[0, own_rows, :], held[1, rows, :], (((1,), (1,)), ((), ())),
+            preferred_element_type=jnp.float32,
+        )
+        own_part[1, block] = lax.dot_general(
+            held[1, own_rows, :], held[0, rows, :], (((1,), (1,)), ((), ())),
+            preferred_element_type=jnp.float32,
+        )
+
+    swap = pltpu.make_async_remote_copy(
+        src_ref=own_part, dst_ref=other_part, send_sem=score_sem.at[0], recv_sem=score_sem.at[1],
+        device_id={"sub": 1 - side}, device_id_type=pl.DeviceIdType.MESH,
+    )
+    swap.start()
+    for step in range(1, owners):
+        block = (me + step) % owners
+        pltpu.make_async_remote_copy(
+            src_ref=turned_all.at[block], dst_ref=turned_all.at[block],
+            send_sem=neg_send.at[step], recv_sem=neg_recv.at[block],
+            device_id={"blk": block}, device_id_type=pl.DeviceIdType.MESH,
+        ).wait_recv()
+    swap.wait()
+
+    down_index = lax.broadcasted_iota(jnp.int32, (row_count, row_count), 0)
+    across_index = lax.broadcasted_iota(jnp.int32, (row_count, row_count), 1)
+
+    @pl.loop(0, owners)
+    def _(block):
+        gap = (block - me + HALF + owners) % owners
+        near = (jnp.zeros((row_count, row_count), jnp.int32) + gap) <= 2 * HALF
+        diagonal = (down_index + me * row_count == across_index + block * row_count).astype(
+            jnp.float32
+        )
+        row_counts = jnp.zeros((row_count, row_count), jnp.float32)
+        col_counts = jnp.zeros((row_count, row_count), jnp.float32)
+        for k in range(neg_count):
+            row_counts += (
+                neg_ref[:, k : k + 1] == across_index + block * row_count
+            ).astype(jnp.float32)
+            col_counts += (
+                turned_all[block, k : k + 1, :] == down_index + me * row_count
+            ).astype(jnp.float32)
+        columns = pl.ds(pl.multiple_of(block * row_count, row_count), row_count)
+        row_w[:, columns] = pair_weights(
+            own_part[0, block] + other_part[0, block], row_counts, near, diagonal, factor
+        )
+        col_w[:, columns] = pair_weights(
+            own_part[1, block] + other_part[1, block], col_counts, near, diagonal, factor
+        )
+
+    @pl.loop(0, width // TILE)
+    def _(tile):
+        columns = pl.ds(pl.multiple_of(tile * TILE, TILE), TILE)
+        gq_ref[:, columns] = (
+            factor
+            * jnp.dot(row_w[...], held[1, :, columns], preferred_element_type=jnp.float32)
+        ).astype(jnp.bfloat16)
+        gp_ref[:, columns] = (
+            factor
+            * jnp.dot(col_w[...], held[0, :, columns], preferred_element_type=jnp.float32)
+        ).astype(jnp.bfloat16)
+
+    for step in range(1, owners):
+        neg_copy(step).wait_send()
+
+    def sent(block, piece, cross):
+        @pl.when((block // 2 <= place) & (place < line - 1))
+        def _():
+            upward(block, piece).wait_send()
+
+        @pl.when((block // 2 >= place) & (place > 0))
+        def _():
+            downward(block, piece).wait_send()
+
+        if cross:
+            across(block, piece).wait_send()
+
+    @pl.loop(0, line)
+    def _(spot):
+        @pl.loop(0, EARLY)
+        def _(piece):
+            sent(spot * 2 + lane, piece, True)
+
+        @pl.loop(EARLY, CHUNKS)
+        def _(piece):
+            sent(spot * 2 + lane, piece, False)
+            sent(spot * 2 + 1 - lane, piece, False)
+
+    @pl.loop(EARLY, CHUNKS)
+    def _(piece):
+        across(me, piece).wait_send()
+
+
+def dense_local(queries, passages, negatives):
+    row_count, width = queries.shape
+    neg_count = negatives.shape[1]
+    owners = lax.axis_size("blk")
+    total = owners * row_count
+    turned = jnp.pad(negatives.T, ((0, 8 - neg_count), (0, 0)), constant_values=-1)
+    out = jax.ShapeDtypeStruct((row_count, width), jnp.bfloat16)
+    vmem = pl.BlockSpec(memory_space=pltpu.VMEM)
+    anywhere = pl.BlockSpec(memory_space=pl.ANY)
+    dma = pltpu.SemaphoreType.DMA
+    return pl.pallas_call(
+        functools.partial(line_kernel, owners, neg_count),
+        out_shape=(out, out),
+        in_specs=[anywhere, anywhere, vmem, vmem],
+        out_specs=(vmem, vmem),
+        scratch_shapes=[
+            pltpu.VMEM((2, total, width), jnp.bfloat16),
+            pltpu.VMEM((owners, 8, row_count), jnp.int32),
+            pltpu.VMEM((2, owners, row_count, row_count), jnp.float32),
+            pltpu.VMEM((2, owners, row_count, row_count), jnp.float32),
+            pltpu.VMEM((row_count, total), jnp.bfloat16),
+            pltpu.VMEM((row_count, total), jnp.bfloat16),
+            dma((2,)),
+            dma((owners,)),
+            dma((owners,)),
+            dma((owners, CHUNKS)),
+            dma((owners, CHUNKS)),
+            dma((owners, CHUNKS)),
+            dma((owners, CHUNKS)),
+            dma((2,)),
+        ],
+        compiler_params=pltpu.CompilerParams(
+            collective_id=0, has_side_effects=True, vmem_limit_bytes=48 * 1024 * 1024
+        ),
+        cost_estimate=pl.CostEstimate(
+            flops=8 * row_count * total * width,
+            bytes_accessed=8 * row_count * width,
+            transcendentals=2 * row_count * total,
+        ),
+    )(queries, passages, negatives, turned)
+
+
 def solution(mesh):
+    owners = mesh.shape["blk"]
+    body = dense_local if owners == 8 else local
     return jax.shard_map(
-        local,
+        body,
         mesh=mesh,
         in_specs=(
             P(("groups", "blk"), "sub"),

time: 415 us -> 108 us (0.26)
  waiting for transfers between devices: 275 us -> 0 us
  Pallas kernels: 0 us -> 102 us
  local copies, waits for them, and re-layouts: 43.7 us -> 4.54 us
  starting transfers between devices: 36 us -> 0 us
  matrix products: 24.5 us -> 0 us
  other arithmetic: 18.7 us -> 0 us
  between operations: 14.3 us -> 0.65 us
    ppermute x9 -> x0, waiting for transfers between devices: 154 us -> none  [shifted(): return lax.ppermute(value, axis, pairs)]
    pallas_call x0 -> x1, Pallas kernels: none -> 102 us  [dense_local(): pl.pallas_call(functools.partial(line_kernel, owners, neg_count), out_sha...]
    all_to_all x3 -> x0, waiting for transfers between devices: 82 us -> none  [the longest x1 82 us: local(): lax.all_to_all(query_buffer, 'blk', split_axis=0, concat_axis=0, tiled=True)]
    psum x1 -> x0, waiting for transfers between devices: 39.4 us -> none  [tile_step(): scores = lax.psum(partial_value, 'sub')]
    gather x4 -> x0, local copies, waits for them, and re-layouts: 29.8 us -> none  [the longest x2 17.6 us: local(): jnp.take(fetched.reshape(owners * capacity, width), slot_index, axis=0)]
    dot_general x18 -> x0, matrix products: 24.5 us -> none  [the longest x5 6.61 us: tile_step(): jnp.einsum('ij,id->jd', coeffs, queries, preferred_element_type=jnp.float32)]
    all_to_all x3 -> x0, starting transfers between devices: 18 us -> none  [the longest x1 7.28 us: local(): lax.all_to_all(requests, 'blk', split_axis=0, concat_axis=0, tiled=True)]
    ppermute x9 -> x0, starting transfers between devices: 18 us -> none  [shifted(): return lax.ppermute(value, axis, pairs)]
  transfers between devices with their start and end apart: 13 -> 0, of which waited for: 8 -> 0; matrix products, arithmetic and copies ran while one was open for 18% -> 0% of each run, Pallas kernels for 0% -> 0%
where the time goes in v2:
time: 108 us
  Pallas kernels  102 us (94%)
  local copies, waits for them, and re-layouts  4.54 us (4%)
    pallas_call x1, Pallas kernels, dense_local(): pl.pallas_call(functools.partial(line_kernel, owners, neg_count), out_sha...  102 us
    unnamed x9, local copies, waits for them, and re-layouts  3.78 us

profile of v2, /device:TPU:0, one launch (start us, length us, event | category | flops | bytes accessed | tf_op | source)
XLA Modules:
  0.0 107.7 jit_solution(16420658451250137729)
XLA Ops:
  0.6 0.0 copy-start.2
  0.6 0.8 pad.4.turned_ref
  1.4 0.0 copy-done.2
  1.4 0.1 copy.5.neg_ref
  1.5 0.0 copy-start
  1.5 1.0 copy-done
  2.6 0.0 copy-start.1
  2.6 1.0 copy-done.1
  3.6 102.5 %shard_map.50 = (bf16[128,2048]{1,0:T(8,128)(2,1)S(1)}, bf16[128,2048]{1,0:T(8,128)(2,1)S(1)}) custom-call(bf16[128,2048]{1,0:T(8,128)(2,1)S(1)} %copy-done, bf16[128,2048]{1,0:T(8,128)(2,1)S(1)} %copy-done.1, s32[128,7]{1,0:T(8,128)S(1)} %copy.5.neg_ref, s32[8,128]{1,0:T(8,128)S(1)} %pad.4.turned_ref), custom_call_target="tpu_custom_call" | custom-call | flops 2147483648 | bytes 2097152 | tf_op jit(solution)/shard_map/pallas_call | solution.py:387
  106.1 0.8 copy.8
  106.9 0.8 copy.9
Async XLA Ops:
  0.6 0.8 copy-start.2
  1.5 1.0 copy-start
  2.6 1.0 copy-start.1

commit v3 on v0

--- a/solution.py
+++ b/solution.py
@@ -1,8 +1,11 @@
+import functools
 import math
 
 import jax
 import jax.numpy as jnp
 from jax import lax
+from jax.experimental import pallas as pl
+from jax.experimental.pallas import tpu as pltpu
 from jax.sharding import PartitionSpec as P
 
 D = 4096
@@ -121,9 +124,376 @@
     return (grad_queries, grad_passages)
 
 
+def pair_weights(scores, counts, near, diagonal, factor):
+    gate = jax.nn.sigmoid(factor * scores + LOGIT_SHIFT)
+    window = jnp.where(near, gate - diagonal, 0.0).astype(jnp.bfloat16).astype(jnp.float32)
+    hard = (HARD_WEIGHT * gate).astype(jnp.bfloat16).astype(jnp.float32)
+    return window + counts * hard
+
+
+PIECES = 4
+
+
+def grid_kernel(
+    owners, neg_count, q_hbm, p_hbm, turned_ref, gq_ref, gp_ref,
+    held, pair, turned_all, own_part, other_part, row_w, col_w, part,
+    run_up, run_down, got_up, got_down, pass_out, pass_in,
+    load_sem, neg_send, neg_recv, pair_sem, swap_send, swap_recv,
+    up_send, down_send, held_recv,
+    sum_up_send, sum_up_recv, sum_down_send, sum_down_recv, pass_send, pass_recv,
+):
+    factor = LOGIT_SLOPE / math.sqrt(D)
+    row_count, width = q_hbm.shape
+    line = owners // 2
+    piece_rows = row_count // PIECES
+    piece_cols = width // PIECES
+    last = line - 1
+    me = lax.axis_index("blk")
+    side = lax.axis_index("sub")
+    place = me // 2
+    lane = me % 2
+    partner = place * 2 + 1 - lane
+
+    def remote(src, dst, send_sem, recv_sem, target):
+        return pltpu.make_async_remote_copy(
+            src_ref=src, dst_ref=dst, send_sem=send_sem, recv_sem=recv_sem,
+            device_id=target, device_id_type=pl.DeviceIdType.MESH,
+        )
+
+    def rows_copy(spot, piece, sems, target):
+        rows = pl.ds(pl.multiple_of(piece * piece_rows, piece_rows), piece_rows)
+        ref = held.at[spot, rows, :]
+        return remote(ref, ref, sems.at[spot, piece], held_recv.at[spot, piece], {"blk": target})
+
+    def rows_up(spot, piece):
+        return rows_copy(spot, piece, up_send, me + 2)
+
+    def rows_down(spot, piece):
+        return rows_copy(spot, piece, down_send, me - 2)
+
+    def sum_up(spot, piece):
+        return remote(
+            run_up.at[spot, piece], got_up.at[spot, piece],
+            sum_up_send.at[spot, piece], sum_up_recv.at[spot, piece], {"blk": me + 2},
+        )
+
+    def sum_down(spot, piece):
+        return remote(
+            run_down.at[spot, piece], got_down.at[spot, piece],
+            sum_down_send.at[spot, piece], sum_down_recv.at[spot, piece], {"blk": me - 2},
+        )
+
+    def pass_copy(piece):
+        return remote(
+            pass_out.at[piece], pass_in.at[piece],
+            pass_send.at[piece], pass_recv.at[piece], {"blk": partner},
+        )
+
+    def pair_copy(which):
+        return remote(
+            pair.at[which], pair.at[which], pair_sem.at[0], pair_sem.at[1], {"blk": partner}
+        )
+
+    def swap(spot):
+        return remote(
+            own_part.at[spot], other_part.at[spot],
+            swap_send.at[spot], swap_recv.at[spot], {"sub": 1 - side},
+        )
+
+    def neg_copy(step, spot):
+        target = ((place + step) % line) * 2 + lane
+        return remote(
+            turned_all.at[spot], turned_all.at[spot],
+            neg_send.at[step], neg_recv.at[spot], {"blk": target},
+        )
+
+    loads = [
+        pltpu.make_async_copy(q_hbm, held.at[place], load_sem.at[0]),
+        pltpu.make_async_copy(p_hbm, pair.at[lane], load_sem.at[1]),
+    ]
+    for load in loads:
+        load.start()
+    barrier = pltpu.get_barrier_semaphore()
+    for step in range(1, line):
+        pl.semaphore_signal(
+            barrier, inc=1, device_id={"blk": ((place + step) % line) * 2 + lane},
+            device_id_type=pl.DeviceIdType.MESH,
+        )
+    pl.semaphore_signal(
+        barrier, inc=1, device_id={"blk": partner}, device_id_type=pl.DeviceIdType.MESH
+    )
+    pl.semaphore_signal(
+        barrier, inc=1, device_id={"sub": 1 - side}, device_id_type=pl.DeviceIdType.MESH
+    )
+    turned_all[place] = turned_ref[...]
+    for load in loads:
+        load.wait()
+    pl.semaphore_wait(barrier, line + 1)
+
+    pair_copy(lane).start()
+
+    @pl.loop(0, PIECES)
+    def _(piece):
+        @pl.when(place < last)
+        def _():
+            rows_up(place, piece).start()
+
+        @pl.when(place > 0)
+        def _():
+            rows_down(place, piece).start()
+
+    for step in range(1, line):
+        neg_copy(step, place).start()
+
+    down_index = lax.broadcasted_iota(jnp.int32, (row_count, row_count), 0)
+    across_index = lax.broadcasted_iota(jnp.int32, (row_count, row_count), 1)
+
+    def score(spot):
+        own_part[spot] = lax.dot_general(
+            pair[...].reshape(2 * row_count, width), held[spot], (((1,), (1,)), ((), ())),
+            preferred_element_type=jnp.float32,
+        )
+        swap(spot).start()
+
+    def product(spot):
+        swap(spot).wait()
+        query_block = spot * 2 + lane
+        for which in range(2):
+            passage_block = place * 2 + which
+            gap = (passage_block - query_block + HALF + owners) % owners
+            near = (jnp.zeros((row_count, row_count), jnp.int32) + gap) <= 2 * HALF
+            passage = down_index + passage_block * row_count
+            diagonal = (passage == across_index + query_block * row_count).astype(jnp.float32)
+            counts = jnp.zeros((row_count, row_count), jnp.float32)
+            for k in range(neg_count):
+                counts += (turned_all[spot, k : k + 1, :] == passage).astype(jnp.float32)
+            rows = slice(which * row_count, (which + 1) * row_count)
+            weights = pair_weights(
+                own_part[spot, rows] + other_part[spot, rows], counts, near, diagonal, factor
+            )
+            columns = pl.ds(pl.multiple_of(spot * row_count, row_count), row_count)
+            col_w[which, :, columns] = weights.astype(jnp.bfloat16)
+            row_w[:, rows] = weights.T.astype(jnp.bfloat16)
+
+        for piece in range(PIECES):
+            columns = slice(piece * piece_cols, (piece + 1) * piece_cols)
+            part[spot, piece] = jnp.dot(
+                row_w[...], pair[:, :, columns].reshape(2 * row_count, piece_cols),
+                preferred_element_type=jnp.float32,
+            )
+
+    def passage_sum(which, piece):
+        columns = pl.ds(pl.multiple_of(piece * piece_cols, piece_cols), piece_cols)
+        return jnp.dot(
+            col_w[which], held[:, :, columns].reshape(line * row_count, piece_cols),
+            preferred_element_type=jnp.float32,
+        )
+
+    def send_passage_sums():
+        @pl.loop(0, PIECES)
+        def _(piece):
+            pass_out[piece] = passage_sum(1 - lane, piece).astype(jnp.bfloat16)
+            pass_copy(piece).start()
+
+    for far in range(1, line):
+        @pl.loop(0, PIECES)
+        def _(piece):
+            @pl.when(place >= far)
+            def _():
+                rows_up(place - far, piece).wait_recv()
+
+                @pl.when(place < last)
+                def _():
+                    rows_up(place - far, piece).start()
+
+            @pl.when(place + far < line)
+            def _():
+                rows_down(place + far, piece).wait_recv()
+
+                @pl.when(place > 0)
+                def _():
+                    rows_down(place + far, piece).start()
+
+        if far == 1:
+            pair_copy(1 - lane).wait_recv()
+
+        below = place - far
+        above = place + far
+        for spot, ready in ((below, place >= far), (above, place + far < line)):
+            @pl.when(ready)
+            def _():
+                score(spot)
+
+        for spot, ready in ((below, place >= far), (above, place + far < line)):
+            @pl.when(ready)
+            def _():
+                neg_copy(1, spot).wait_recv()
+                product(spot)
+
+        inner = (place > 0) & (place < last)
+        if far == line - 1:
+            @pl.when(inner)
+            def _():
+                send_passage_sums()
+
+        @pl.loop(0, PIECES)
+        def _(piece):
+            @pl.when(place < far)
+            def _():
+                @pl.when(place == 0)
+                def _():
+                    run_up[far, piece] = part[far, piece].astype(jnp.bfloat16)
+
+                @pl.when(place > 0)
+                def _():
+                    sum_up(far, piece).wait_recv()
+                    run_up[far, piece] = (
+                        part[far, piece] + got_up[far, piece].astype(jnp.float32)
+                    ).astype(jnp.bfloat16)
+
+                sum_up(far, piece).start()
+
+            spot = last - far
+
+            @pl.when(place > spot)
+            def _():
+                @pl.when(place == last)
+                def _():
+                    run_down[spot, piece] = part[spot, piece].astype(jnp.bfloat16)
+
+                @pl.when(place < last)
+                def _():
+                    sum_down(spot, piece).wait_recv()
+                    run_down[spot, piece] = (
+                        part[spot, piece] + got_down[spot, piece].astype(jnp.float32)
+                    ).astype(jnp.bfloat16)
+
+                sum_down(spot, piece).start()
+
+        if far == 1:
+            score(place)
+            product(place)
+
+        if far == line - 1:
+            @pl.when(jnp.logical_not(inner))
+            def _():
+                send_passage_sums()
+
+    @pl.loop(0, PIECES)
+    def _(piece):
+        columns = pl.ds(pl.multiple_of(piece * piece_cols, piece_cols), piece_cols)
+
+        @pl.when(place > 0)
+        def _():
+            sum_up(place, piece).wait_recv()
+            part[place, piece] += got_up[place, piece].astype(jnp.float32)
+
+        @pl.when(place < last)
+        def _():
+            sum_down(place, piece).wait_recv()
+            part[place, piece] += got_down[place, piece].astype(jnp.float32)
+
+        gq_ref[:, columns] = (factor * part[place, piece]).astype(jnp.bfloat16)
+
+    @pl.loop(0, PIECES)
+    def _(piece):
+        columns = pl.ds(pl.multiple_of(piece * piece_cols, piece_cols), piece_cols)
+        mine = passage_sum(lane, piece)
+        pass_copy(piece).wait_recv()
+        gp_ref[:, columns] = (
+            factor * (mine + pass_in[piece].astype(jnp.float32))
+        ).astype(jnp.bfloat16)
+
+    pair_copy(lane).wait_send()
+    for step in range(1, line):
+        neg_copy(step, place).wait_send()
+
+    @pl.loop(0, PIECES)
+    def _(piece):
+        pass_copy(piece).wait_send()
+        for spot in range(line):
+            @pl.when((place >= spot) & (place < last))
+            def _():
+                rows_up(spot, piece).wait_send()
+
+            @pl.when((place <= spot) & (place > 0))
+            def _():
+                rows_down(spot, piece).wait_send()
+
+            @pl.when(place < spot)
+            def _():
+                sum_up(spot, piece).wait_send()
+
+            @pl.when(place > spot)
+            def _():
+                sum_down(spot, piece).wait_send()
+
+
+def dense_local(queries, passages, negatives):
+    row_count, width = queries.shape
+    neg_count = negatives.shape[1]
+    owners = lax.axis_size("blk")
+    line = owners // 2
+    piece_cols = width // PIECES
+    turned = jnp.pad(negatives.T, ((0, 8 - neg_count), (0, 0)), constant_values=-1)
+    out = jax.ShapeDtypeStruct((row_count, width), jnp.bfloat16)
+    vmem = pl.BlockSpec(memory_space=pltpu.VMEM)
+    anywhere = pl.BlockSpec(memory_space=pl.ANY)
+    dma = pltpu.SemaphoreType.DMA
+    sums = pltpu.VMEM((line, PIECES, row_count, piece_cols), jnp.bfloat16)
+    grid = dma((line, PIECES))
+    return pl.pallas_call(
+        functools.partial(grid_kernel, owners, neg_count),
+        out_shape=(out, out),
+        in_specs=[anywhere, anywhere, vmem],
+        out_specs=(vmem, vmem),
+        scratch_shapes=[
+            pltpu.VMEM((line, row_count, width), jnp.bfloat16),
+            pltpu.VMEM((2, row_count, width), jnp.bfloat16),
+            pltpu.VMEM((line, 8, row_count), jnp.int32),
+            pltpu.VMEM((line, 2 * row_count, row_count), jnp.float32),
+            pltpu.VMEM((line, 2 * row_count, row_count), jnp.float32),
+            pltpu.VMEM((row_count, 2 * row_count), jnp.bfloat16),
+            pltpu.VMEM((2, row_count, line * row_count), jnp.bfloat16),
+            pltpu.VMEM((line, PIECES, row_count, piece_cols), jnp.float32),
+            sums,
+            sums,
+            sums,
+            sums,
+            pltpu.VMEM((PIECES, row_count, piece_cols), jnp.bfloat16),
+            pltpu.VMEM((PIECES, row_count, piece_cols), jnp.bfloat16),
+            dma((2,)),
+            dma((line,)),
+            dma((line,)),
+            dma((2,)),
+            dma((line,)),
+            dma((line,)),
+            grid,
+            grid,
+            grid,
+            grid,
+            grid,
+            grid,
+            grid,
+            dma((PIECES,)),
+            dma((PIECES,)),
+        ],
+        compiler_params=pltpu.CompilerParams(
+            collective_id=0, has_side_effects=True, vmem_limit_bytes=60 * 1024 * 1024
+        ),
+        cost_estimate=pl.CostEstimate(
+            flops=12 * row_count * row_count * owners * width // 2,
+            bytes_accessed=8 * row_count * width,
+            transcendentals=row_count * row_count * owners,
+        ),
+    )(queries, passages, turned)
+
+
 def solution(mesh):
+    owners = mesh.shape["blk"]
+    body = dense_local if owners == 8 else local
     return jax.shard_map(
-        local,
+        body,
         mesh=mesh,
         in_specs=(
             P(("groups", "blk"), "sub"),

time: 415 us -> 93.8 us (0.23)
  waiting for transfers between devices: 275 us -> 0 us
  Pallas kernels: 0 us -> 88.9 us
  local copies, waits for them, and re-layouts: 43.7 us -> 4.02 us
  starting transfers between devices: 36 us -> 0 us
  matrix products: 24.5 us -> 0 us
  other arithmetic: 18.7 us -> 0 us
  between operations: 14.3 us -> 0.65 us
    ppermute x9 -> x0, waiting for transfers between devices: 154 us -> none  [shifted(): return lax.ppermute(value, axis, pairs)]
    pallas_call x0 -> x1, Pallas kernels: none -> 88.9 us  [dense_local(): pl.pallas_call(functools.partial(grid_kernel, owners, neg_count), out_sha...]
    all_to_all x3 -> x0, waiting for transfers between devices: 82 us -> none  [the longest x1 82 us: local(): lax.all_to_all(query_buffer, 'blk', split_axis=0, concat_axis=0, tiled=True)]
    psum x1 -> x0, waiting for transfers between devices: 39.4 us -> none  [tile_step(): scores = lax.psum(partial_value, 'sub')]
    gather x4 -> x0, local copies, waits for them, and re-layouts: 29.8 us -> none  [the longest x2 17.6 us: local(): jnp.take(fetched.reshape(owners * capacity, width), slot_index, axis=0)]
    dot_general x18 -> x0, matrix products: 24.5 us -> none  [the longest x5 6.61 us: tile_step(): jnp.einsum('ij,id->jd', coeffs, queries, preferred_element_type=jnp.float32)]
    all_to_all x3 -> x0, starting transfers between devices: 18 us -> none  [the longest x1 7.28 us: local(): lax.all_to_all(requests, 'blk', split_axis=0, concat_axis=0, tiled=True)]
    ppermute x9 -> x0, starting transfers between devices: 18 us -> none  [shifted(): return lax.ppermute(value, axis, pairs)]
  transfers between devices with their start and end apart: 13 -> 0, of which waited for: 8 -> 0; matrix products, arithmetic and copies ran while one was open for 18% -> 0% of each run, Pallas kernels for 0% -> 0%
where the time goes in v3:
time: 93.8 us; the launch traced here: 93.6 us
  Pallas kernels  88.9 us (95%)
  local copies, waits for them, and re-layouts  4.02 us (4%)
    pallas_call x1, Pallas kernels, dense_local(): pl.pallas_call(functools.partial(grid_kernel, owners, neg_count), out_sha...  88.9 us
    unnamed x4, local copies, waits for them, and re-layouts  2.74 us

profile of v3, /device:TPU:0, one launch (start us, length us, event | category | flops | bytes accessed | tf_op | source)
XLA Modules:
  0.0 93.6 jit_solution(10965466400643032723)
XLA Ops:
  0.6 1.3 %pad.4.turned_ref = s32[8,128]{1,0:T(8,128)} pad(s32[7,128]{1,0:T(8,128)} %bitcast.1, s32[]{:T(128)} %constant.0.clone.1), padding=0_1x0_0 | pad | bytes 7684 | tf_op jit(solution)/shard_map/jit(_pad)/pad | solution.py:438
  1.9 88.9 %shard_map.50 = (bf16[128,2048]{1,0:T(8,128)(2,1)}, bf16[128,2048]{1,0:T(8,128)(2,1)}) custom-call(bf16[128,2048]{1,0:T(8,128)(2,1)} %q_hbm.1, bf16[128,2048]{1,0:T(8,128)(2,1)} %p_hbm.1, s32[8,128]{1,0:T(8,128)} %pad.4.turned_ref), custom_call_target="tpu_custom_call" | custom-call | flops 1610612736 | bytes 2097152 | tf_op jit(solution)/shard_map/pallas_call | solution.py:445
  90.9 0.0 copy-start
  90.9 1.9 %copy.7 = bf16[128,2048]{1,0:T(8,128)(2,1)} copy(bf16[128,2048]{1,0:T(8,128)(2,1)} %get-tuple-element.4) | data formatting | bytes 1048576
  92.8 0.0 copy-done
  92.8 0.8 copy.8
Async XLA Ops:
  90.9 2.0 %copy-start = (bf16[128,2048]{1,0:T(8,128)(2,1)S(1)}, bf16[128,2048]{1,0:T(8,128)(2,1)}, u32[]{:S(2)}) copy-start(bf16[128,2048]{1,0:T(8,128)(2,1)} %get-tuple-element.5) | copy-start | bytes 1572868

commit v4 on v3

--- a/solution.py
+++ b/solution.py
@@ -132,6 +132,8 @@
 
 
 PIECES = 4
+ROW_PIECES = 4
+LAG = 1
 
 
 def grid_kernel(
@@ -145,7 +147,7 @@
     factor = LOGIT_SLOPE / math.sqrt(D)
     row_count, width = q_hbm.shape
     line = owners // 2
-    piece_rows = row_count // PIECES
+    piece_rows = row_count // ROW_PIECES
     piece_cols = width // PIECES
     last = line - 1
     me = lax.axis_index("blk")
@@ -232,7 +234,7 @@
 
     pair_copy(lane).start()
 
-    @pl.loop(0, PIECES)
+    @pl.loop(0, ROW_PIECES)
     def _(piece):
         @pl.when(place < last)
         def _():
@@ -296,7 +298,7 @@
             pass_copy(piece).start()
 
     for far in range(1, line):
-        @pl.loop(0, PIECES)
+        @pl.loop(0, ROW_PIECES)
         def _(piece):
             @pl.when(place >= far)
             def _():
@@ -331,14 +333,19 @@
                 product(spot)
 
         inner = (place > 0) & (place < last)
-        if far == line - 1:
+        if far == line - 2:
             @pl.when(inner)
             def _():
                 send_passage_sums()
 
-        @pl.loop(0, PIECES)
-        def _(piece):
-            @pl.when(place < far)
+        spot = last - far
+        low = place * 2 < line
+
+        @pl.loop(0, PIECES + LAG)
+        def _(step):
+            piece = step - jnp.where(low, 0, LAG)
+
+            @pl.when((place < far) & (piece >= 0) & (piece < PIECES))
             def _():
                 @pl.when(place == 0)
                 def _():
@@ -353,22 +360,22 @@
 
                 sum_up(far, piece).start()
 
-            spot = last - far
-
-            @pl.when(place > spot)
+            other = step - jnp.where(low, LAG, 0)
+
+            @pl.when((place > spot) & (other >= 0) & (other < PIECES))
             def _():
                 @pl.when(place == last)
                 def _():
-                    run_down[spot, piece] = part[spot, piece].astype(jnp.bfloat16)
+                    run_down[spot, other] = part[spot, other].astype(jnp.bfloat16)
 
                 @pl.when(place < last)
                 def _():
-                    sum_down(spot, piece).wait_recv()
-                    run_down[spot, piece] = (
-                        part[spot, piece] + got_down[spot, piece].astype(jnp.float32)
+                    sum_down(spot, other).wait_recv()
+                    run_down[spot, other] = (
+                        part[spot, other] + got_down[spot, other].astype(jnp.float32)
                     ).astype(jnp.bfloat16)
 
-                sum_down(spot, piece).start()
+                sum_down(spot, other).start()
 
         if far == 1:
             score(place)
@@ -408,18 +415,21 @@
     for step in range(1, line):
         neg_copy(step, place).wait_send()
 
+    @pl.loop(0, ROW_PIECES)
+    def _(piece):
+        for spot in range(line):
+            @pl.when((place >= spot) & (place < last))
+            def _():
+                rows_up(spot, piece).wait_send()
+
+            @pl.when((place <= spot) & (place > 0))
+            def _():
+                rows_down(spot, piece).wait_send()
+
     @pl.loop(0, PIECES)
     def _(piece):
         pass_copy(piece).wait_send()
         for spot in range(line):
-            @pl.when((place >= spot) & (place < last))
-            def _():
-                rows_up(spot, piece).wait_send()
-
-            @pl.when((place <= spot) & (place > 0))
-            def _():
-                rows_down(spot, piece).wait_send()
-
             @pl.when(place < spot)
             def _():
                 sum_up(spot, piece).wait_send()
@@ -442,6 +452,7 @@
     dma = pltpu.SemaphoreType.DMA
     sums = pltpu.VMEM((line, PIECES, row_count, piece_cols), jnp.bfloat16)
     grid = dma((line, PIECES))
+    row_grid = dma((line, ROW_PIECES))
     return pl.pallas_call(
         functools.partial(grid_kernel, owners, neg_count),
         out_shape=(out, out),
@@ -468,9 +479,9 @@
             dma((2,)),
             dma((line,)),
             dma((line,)),
-            grid,
-            grid,
-            grid,
+            row_grid,
+            row_grid,
+            row_grid,
             grid,
             grid,
             grid,

time: 93.8 us -> 75.8 us (0.81)
  Pallas kernels: 88.9 us -> 70.9 us
    pallas_call x1, Pallas kernels: 88.9 us -> 70.9 us  [dense_local(): pl.pallas_call(functools.partial(grid_kernel, owners, neg_count), out_sha...]
where the time goes in v4:
time: 75.8 us; the launch traced here: 75.6 us
  Pallas kernels  70.9 us (94%)
  local copies, waits for them, and re-layouts  4.02 us (5%)
    pallas_call x1, Pallas kernels, dense_local(): pl.pallas_call(functools.partial(grid_kernel, owners, neg_count), out_sha...  70.9 us
    unnamed x4, local copies, waits for them, and re-layouts  2.74 us

profile of v4, /device:TPU:0, one launch (start us, length us, event | category | flops | bytes accessed | tf_op | source)
XLA Modules:
  0.0 75.6 jit_solution(15685470549204967595)
XLA Ops:
  0.6 1.3 %pad.4.turned_ref = s32[8,128]{1,0:T(8,128)} pad(s32[7,128]{1,0:T(8,128)} %bitcast.1, s32[]{:T(128)} %constant.0.clone.1), padding=0_1x0_0 | pad | bytes 7684 | tf_op jit(solution)/shard_map/jit(_pad)/pad | solution.py:448
  1.9 70.9 %shard_map.50 = (bf16[128,2048]{1,0:T(8,128)(2,1)}, bf16[128,2048]{1,0:T(8,128)(2,1)}) custom-call(bf16[128,2048]{1,0:T(8,128)(2,1)} %q_hbm.1, bf16[128,2048]{1,0:T(8,128)(2,1)} %p_hbm.1, s32[8,128]{1,0:T(8,128)} %pad.4.turned_ref), custom_call_target="tpu_custom_call" | custom-call | flops 1610612736 | bytes 2097152 | tf_op jit(solution)/shard_map/pallas_call | solution.py:456
  72.8 0.0 copy-start
  72.8 1.9 %copy.7 = bf16[128,2048]{1,0:T(8,128)(2,1)} copy(bf16[128,2048]{1,0:T(8,128)(2,1)} %get-tuple-element.4) | data formatting | bytes 1048576
  74.8 0.0 copy-done
  74.8 0.8 %copy.8 = bf16[128,2048]{1,0:T(8,128)(2,1)} copy(bf16[128,2048]{1,0:T(8,128)(2,1)S(1)} %copy-done) | data formatting | bytes 1048576
Async XLA Ops:
  72.8 2.0 %copy-start = (bf16[128,2048]{1,0:T(8,128)(2,1)S(1)}, bf16[128,2048]{1,0:T(8,128)(2,1)}, u32[]{:S(2)}) copy-start(bf16[128,2048]{1,0:T(8,128)(2,1)} %get-tuple-element.5) | copy-start | bytes 1572868

commit v5 on v4

--- a/solution.py
+++ b/solution.py
@@ -131,9 +131,9 @@
     return window + counts * hard
 
 
-PIECES = 4
+PIECES = 8
 ROW_PIECES = 4
-LAG = 1
+LAG = 2
 
 
 def grid_kernel(
@@ -389,27 +389,27 @@
     @pl.loop(0, PIECES)
     def _(piece):
         columns = pl.ds(pl.multiple_of(piece * piece_cols, piece_cols), piece_cols)
-
-        @pl.when(place > 0)
-        def _():
-            sum_up(place, piece).wait_recv()
-            part[place, piece] += got_up[place, piece].astype(jnp.float32)
-
-        @pl.when(place < last)
-        def _():
-            sum_down(place, piece).wait_recv()
-            part[place, piece] += got_down[place, piece].astype(jnp.float32)
-
-        gq_ref[:, columns] = (factor * part[place, piece]).astype(jnp.bfloat16)
-
-    @pl.loop(0, PIECES)
-    def _(piece):
-        columns = pl.ds(pl.multiple_of(piece * piece_cols, piece_cols), piece_cols)
         mine = passage_sum(lane, piece)
         pass_copy(piece).wait_recv()
         gp_ref[:, columns] = (
             factor * (mine + pass_in[piece].astype(jnp.float32))
         ).astype(jnp.bfloat16)
+
+    @pl.loop(0, PIECES)
+    def _(piece):
+        columns = pl.ds(pl.multiple_of(piece * piece_cols, piece_cols), piece_cols)
+
+        @pl.when(place > 0)
+        def _():
+            sum_up(place, piece).wait_recv()
+            part[place, piece] += got_up[place, piece].astype(jnp.float32)
+
+        @pl.when(place < last)
+        def _():
+            sum_down(place, piece).wait_recv()
+            part[place, piece] += got_down[place, piece].astype(jnp.float32)
+
+        gq_ref[:, columns] = (factor * part[place, piece]).astype(jnp.bfloat16)
 
     pair_copy(lane).wait_send()
     for step in range(1, line):
@@ -445,7 +445,7 @@
     owners = lax.axis_size("blk")
     line = owners // 2
     piece_cols = width // PIECES
-    turned = jnp.pad(negatives.T, ((0, 8 - neg_count), (0, 0)), constant_values=-1)
+    turned = negatives.T
     out = jax.ShapeDtypeStruct((row_count, width), jnp.bfloat16)
     vmem = pl.BlockSpec(memory_space=pltpu.VMEM)
     anywhere = pl.BlockSpec(memory_space=pl.ANY)
@@ -461,7 +461,7 @@
         scratch_shapes=[
             pltpu.VMEM((line, row_count, width), jnp.bfloat16),
             pltpu.VMEM((2, row_count, width), jnp.bfloat16),
-            pltpu.VMEM((line, 8, row_count), jnp.int32),
+            pltpu.VMEM((line, neg_count, row_count), jnp.int32),
             pltpu.VMEM((line, 2 * row_count, row_count), jnp.float32),
             pltpu.VMEM((line, 2 * row_count, row_count), jnp.float32),
             pltpu.VMEM((row_count, 2 * row_count), jnp.bfloat16),

time: 75.8 us -> 72.1 us (0.951)
  Pallas kernels: 70.9 us -> 68.5 us
  local copies, waits for them, and re-layouts: 4.02 us -> 2.74 us
    pallas_call x1, Pallas kernels: 70.9 us -> 68.5 us  [dense_local(): pl.pallas_call(functools.partial(grid_kernel, owners, neg_count), out_sha...]
    pad x1 -> x0, local copies, waits for them, and re-layouts: 1.28 us -> none  [dense_local(): jnp.pad(negatives.T, ((0, 8 - neg_count), (0, 0)), constant_values=-1)]
where the time goes in v5:
time: 72.1 us; the launch traced here: 71.9 us
  Pallas kernels  68.5 us (95%)
  local copies, waits for them, and re-layouts  2.74 us (4%)
    pallas_call x1, Pallas kernels, dense_local(): pl.pallas_call(functools.partial(grid_kernel, owners, neg_count), out_sha...  68.5 us
    unnamed x4, local copies, waits for them, and re-layouts  2.74 us

profile of v5, /device:TPU:0, one launch (start us, length us, event | category | flops | bytes accessed | tf_op | source)
XLA Modules:
  0.0 71.9 jit_solution(4002437285819604339)
XLA Ops:
  0.6 68.5 %shard_map.50 = (bf16[128,2048]{1,0:T(8,128)(2,1)}, bf16[128,2048]{1,0:T(8,128)(2,1)}) custom-call(bf16[128,2048]{1,0:T(8,128)(2,1)} %q_hbm.1, bf16[128,2048]{1,0:T(8,128)(2,1)} %p_hbm.1, s32[7,128]{1,0:T(8,128)} %bitcast.1), custom_call_target="tpu_custom_call" | custom-call | flops 1610612736 | bytes 2097152 | tf_op jit(solution)/shard_map/pallas_call | solution.py:456
  69.2 0.0 copy-start
  69.2 1.9 %copy.7 = bf16[128,2048]{1,0:T(8,128)(2,1)} copy(bf16[128,2048]{1,0:T(8,128)(2,1)} %get-tuple-element.4) | data formatting | bytes 1048576
  71.1 0.0 copy-done
  71.1 0.8 %copy.8 = bf16[128,2048]{1,0:T(8,128)(2,1)} copy(bf16[128,2048]{1,0:T(8,128)(2,1)S(1)} %copy-done) | data formatting | bytes 1048576
Async XLA Ops:
  69.2 2.0 %copy-start = (bf16[128,2048]{1,0:T(8,128)(2,1)S(1)}, bf16[128,2048]{1,0:T(8,128)(2,1)}, u32[]{:S(2)}) copy-start(bf16[128,2048]{1,0:T(8,128)(2,1)} %get-tuple-element.5) | copy-start | bytes 1572868

commit v6 on v5

--- a/solution.py
+++ b/solution.py
@@ -133,7 +133,7 @@
 
 PIECES = 8
 ROW_PIECES = 4
-LAG = 2
+LAG = 3
 
 
 def grid_kernel(
@@ -279,10 +279,21 @@
 
         for piece in range(PIECES):
             columns = slice(piece * piece_cols, (piece + 1) * piece_cols)
-            part[spot, piece] = jnp.dot(
+            tile = jnp.dot(
                 row_w[...], pair[:, :, columns].reshape(2 * row_count, piece_cols),
                 preferred_element_type=jnp.float32,
             )
+            part[spot, piece] = tile
+
+            @pl.when((place == 0) & (spot > 0))
+            def _():
+                run_up[spot, piece] = tile.astype(jnp.bfloat16)
+                sum_up(spot, piece).start()
+
+            @pl.when((place == last) & (spot < last))
+            def _():
+                run_down[spot, piece] = tile.astype(jnp.bfloat16)
+                sum_down(spot, piece).start()
 
     def passage_sum(which, piece):
         columns = pl.ds(pl.multiple_of(piece * piece_cols, piece_cols), piece_cols)
@@ -345,36 +356,22 @@
         def _(step):
             piece = step - jnp.where(low, 0, LAG)
 
-            @pl.when((place < far) & (piece >= 0) & (piece < PIECES))
-            def _():
-                @pl.when(place == 0)
-                def _():
-                    run_up[far, piece] = part[far, piece].astype(jnp.bfloat16)
-
-                @pl.when(place > 0)
-                def _():
-                    sum_up(far, piece).wait_recv()
-                    run_up[far, piece] = (
-                        part[far, piece] + got_up[far, piece].astype(jnp.float32)
-                    ).astype(jnp.bfloat16)
-
+            @pl.when((place > 0) & (place < far) & (piece >= 0) & (piece < PIECES))
+            def _():
+                sum_up(far, piece).wait_recv()
+                run_up[far, piece] = (
+                    part[far, piece] + got_up[far, piece].astype(jnp.float32)
+                ).astype(jnp.bfloat16)
                 sum_up(far, piece).start()
 
             other = step - jnp.where(low, LAG, 0)
 
-            @pl.when((place > spot) & (other >= 0) & (other < PIECES))
-            def _():
-                @pl.when(place == last)
-                def _():
-                    run_down[spot, other] = part[spot, other].astype(jnp.bfloat16)
-
-                @pl.when(place < last)
-                def _():
-                    sum_down(spot, other).wait_recv()
-                    run_down[spot, other] = (
-                        part[spot, other] + got_down[spot, other].astype(jnp.float32)
-                    ).astype(jnp.bfloat16)
-
+            @pl.when((place < last) & (place > spot) & (other >= 0) & (other < PIECES))
+            def _():
+                sum_down(spot, other).wait_recv()
+                run_down[spot, other] = (
+                    part[spot, other] + got_down[spot, other].astype(jnp.float32)
+                ).astype(jnp.bfloat16)
                 sum_down(spot, other).start()
 
         if far == 1:

time: 72.1 us -> 71.5 us (level)
  no operation moved by 1% of the time
where the time goes in v6:
time: 71.5 us; the launch traced here: 71.3 us
  Pallas kernels  67.9 us (95%)
  local copies, waits for them, and re-layouts  2.74 us (4%)
    pallas_call x1, Pallas kernels, dense_local(): pl.pallas_call(functools.partial(grid_kernel, owners, neg_count), out_sha...  67.9 us
    unnamed x4, local copies, waits for them, and re-layouts  2.74 us

profile of v6, /device:TPU:0, one launch (start us, length us, event | category | flops | bytes accessed | tf_op | source)
XLA Modules:
  0.0 71.3 jit_solution(4057488637884951540)
XLA Ops:
  0.6 67.9 %shard_map.50 = (bf16[128,2048]{1,0:T(8,128)(2,1)}, bf16[128,2048]{1,0:T(8,128)(2,1)}) custom-call(bf16[128,2048]{1,0:T(8,128)(2,1)} %q_hbm.1, bf16[128,2048]{1,0:T(8,128)(2,1)} %p_hbm.1, s32[7,128]{1,0:T(8,128)} %bitcast.1), custom_call_target="tpu_custom_call" | custom-call | flops 1610612736 | bytes 2097152 | tf_op jit(solution)/shard_map/pallas_call | solution.py:453
  68.5 0.0 copy-start
  68.6 1.9 %copy.7 = bf16[128,2048]{1,0:T(8,128)(2,1)} copy(bf16[128,2048]{1,0:T(8,128)(2,1)} %get-tuple-element.4) | data formatting | bytes 1048576
  70.5 0.0 copy-done
  70.5 0.8 %copy.8 = bf16[128,2048]{1,0:T(8,128)(2,1)} copy(bf16[128,2048]{1,0:T(8,128)(2,1)S(1)} %copy-done) | data formatting | bytes 1048576
Async XLA Ops:
  68.5 2.0 %copy-start = (bf16[128,2048]{1,0:T(8,128)(2,1)S(1)}, bf16[128,2048]{1,0:T(8,128)(2,1)}, u32[]{:S(2)}) copy-start(bf16[128,2048]{1,0:T(8,128)(2,1)} %get-tuple-element.5) | copy-start | bytes 1572868
